TPU v7x, 32 devices: a whole 2x2x4 slice. The times are simulated.
32 devices in a mesh: dp: 8 (over y, x, core), tensor: 4 (over z).
Axes of the slice: x: 2, y: 2, z: 4, core: 2. Of those that a mesh axis runs over, the one named last changes fastest.
Arguments:
- inputs: bfloat16 [16, 1024, 1024], P('dp', None, 'tensor'), may hold values from -6 to 6
- segment: int32 [16, 1024], P('dp'), may hold values from 0 to 4, as said below
- cotangent: bfloat16 [16, 1024, 1024], P('dp', None, 'tensor'), may hold values from -6 to 6
- norm_gain: float32 [1024], replicated, may hold values from 0.1 to 1.9
- weight_z: bfloat16 [1024, 2048], P(None, 'tensor'), may hold values from -0.1875 to 0.1875
- weight_x: bfloat16 [1024, 2048], P(None, 'tensor'), may hold values from -0.1875 to 0.1875
- weight_bc: bfloat16 [1024, 256], replicated, may hold values from -0.1875 to 0.1875
- weight_dt: bfloat16 [1024, 32], P(None, 'tensor'), may hold values from -0.1875 to 0.1875
- conv_weight_x: float32 [4, 2048], P(None, 'tensor'), may hold values from -3 to 3
- conv_bias_x: float32 [2048], P('tensor'), may hold values from -3 to 3
- conv_weight_bc: float32 [4, 256], replicated, may hold values from -3 to 3
- conv_bias_bc: float32 [256], replicated, may hold values from -3 to 3
- step_bias: float32 [32], P('tensor'), may hold values from -6 to -2
- decay_log: float32 [32], P('tensor'), may hold values from 0 to 2.77
- skip_gain: float32 [32], P('tensor'), may hold values from 0.5 to 2
- gate_gain: float32 [2048], P('tensor'), may hold values from 0.1 to 1.9
- weight_out: bfloat16 [2048, 1024], P('tensor'), may hold values from -0.125 to 0.125
Outputs:
- output: bfloat16 [16, 1024, 1024], P('dp', None, 'tensor')
- input_grad: float32 [16, 1024, 1024], P('dp', None, 'tensor')
- norm_gain_grad: float32 [1024], P('tensor')
- weight_z_grad: float32 [1024, 2048], P('dp', 'tensor')
- weight_x_grad: float32 [1024, 2048], P('dp', 'tensor')
- weight_bc_grad: float32 [1024, 256], P('dp')
- weight_dt_grad: float32 [1024, 32], P('dp', 'tensor')
- conv_weight_x_grad: float32 [4, 2048], P(None, 'tensor')
- conv_bias_x_grad: float32 [2048], P('tensor')
- conv_weight_bc_grad: float32 [4, 256], replicated
- conv_bias_bc_grad: float32 [256], replicated
- step_bias_grad: float32 [32], P('tensor')
- decay_log_grad: float32 [32], P('tensor')
- skip_gain_grad: float32 [32], P('tensor')
- gate_gain_grad: float32 [2048], P('tensor')
- weight_out_grad: float32 [2048, 1024], P('tensor', 'dp')
Inputs may be any that keep to these rules, and one draw needn't show every extreme that they name: `segment`: segment numbers start at 0 in each sequence and never fall along it; a new number starts a new document, where the scan state and the convolution restart. Each sequence holds one document of exactly 800 tokens, at its start or at its end; the inner documents have 60 to 800 tokens, the one at the other end may be shorter.
All inputs are finite; a program needn't handle non-finite values.
Results may differ from a plain program's by a relative error of at most 0.008.
Values may be sent and summed in bfloat16 or wider, within the bound.
No kernel may reach another device: no remote copies, remote signals or barrier semaphores. Data moves between devices by JAX's collectives and lax.ppermute only.
A program may use at most 192 MiB of HBM per device.

v0:
```python
import jax
import jax.numpy as jnp
from jax import lax
from jax.sharding import PartitionSpec as P

SPAN = 256
SEQ_MB = 1
INNER = 2048
eps = 1e-05


def causal_conv(values, weights, biases, segment):
    taps = weights.shape[0]
    total = biases + weights[taps - 1] * values
    for offset in range(1, taps):
        moved = jnp.pad(values, ((0, 0), (offset, 0), (0, 0)))[:, :-offset]
        earlier = jnp.pad(segment, ((0, 0), (offset, 0)), constant_values=-1)[:, :-offset]
        same_doc = (earlier == segment).astype(values.dtype)[..., None]
        total = total + weights[taps - 1 - offset] * moved * same_doc
    return total


def ssd_scan(values, decays, deltas, b_matrix, c_matrix, segment, block_len):
    seq_count, length, head_count, head_size = values.shape
    block_count = length // block_len

    def to_blocks(source):
        shaped = source.reshape((seq_count, block_count, block_len) + source.shape[2:])
        return jnp.moveaxis(shaped, 1, 0)

    pieces = tuple(
        (to_blocks(source) for source in (values, decays, deltas, b_matrix, c_matrix, segment))
    )
    state_init = jnp.zeros((seq_count, head_count, b_matrix.shape[-1], head_size), values.dtype)
    prev_init = jnp.full((seq_count,), -1, jnp.int32)
    lower_tri = jnp.arange(block_len)[:, None] >= jnp.arange(block_len)[None, :]

    def advance(carried_in, block_in):
        prior_state, previous = carried_in
        value_blk, decay_blk, delta_blk, b_blk, c_blk, seg_blk = block_in
        cumulative = jnp.cumsum(decay_blk, axis=1)
        allowed = (seg_blk[:, :, None] == seg_blk[:, None, :]) & lower_tri[None]
        masking = allowed.astype(values.dtype)[..., None]
        spread = cumulative[:, :, None, :] - cumulative[:, None, :, :]
        kernel = jnp.exp(jnp.where(allowed[..., None], spread, 0.0)) * masking
        scores = jnp.einsum("stn,sun->stu", c_blk, b_blk, precision=lax.Precision.HIGHEST)
        mixing = scores[..., None] * kernel * delta_blk[:, None, :, :]
        inside = jnp.einsum("stuh,suhp->sthp", mixing, value_blk, precision=lax.Precision.HIGHEST)
        final_seg = seg_blk[:, -1]
        same_end = (seg_blk == final_seg[:, None]).astype(values.dtype)[..., None]
        tail_weight = jnp.exp(cumulative[:, -1:, :] - cumulative) * same_end * delta_blk
        local_state = jnp.einsum(
            "sun,suhp->shnp",
            b_blk,
            tail_weight[..., None] * value_blk,
            precision=lax.Precision.HIGHEST,
        )
        entering = (
            jnp.exp(cumulative) * (seg_blk == previous[:, None]).astype(values.dtype)[..., None]
        )
        outside = (
            jnp.einsum("stn,shnp->sthp", c_blk, prior_state, precision=lax.Precision.HIGHEST)
            * entering[..., None]
        )
        carried = (
            jnp.exp(cumulative[:, -1, :]) * (final_seg == previous).astype(values.dtype)[:, None]
        )
        new_state = carried[:, :, None, None] * prior_state + local_state
        return ((new_state, final_seg), inside + outside)

    _, results = lax.scan(jax.checkpoint(advance), (state_init, prev_init), pieces)
    return jnp.moveaxis(results, 0, 1).reshape(seq_count, length, head_count, head_size)


def mixer(gate_pre, value_pre, bc_pre, delta_pre, params, segment):
    conv_weight_x, conv_bias_x, conv_weight_bc, conv_bias_bc, step_bias, decay_log, skip_gain = (
        params
    )
    conv_value = jax.nn.silu(causal_conv(value_pre, conv_weight_x, conv_bias_x, segment))
    conv_bc = jax.nn.silu(causal_conv(bc_pre, conv_weight_bc, conv_bias_bc, segment))
    state_size = conv_bc.shape[-1] // 2
    deltas = jax.nn.softplus(delta_pre + step_bias)
    decays = -deltas * jnp.exp(decay_log)
    seq_count, length, head_count = deltas.shape
    values = conv_value.reshape(seq_count, length, head_count, -1)
    scan_result = ssd_scan(
        values, decays, deltas, conv_bc[..., :state_size], conv_bc[..., state_size:], segment, SPAN
    )
    scan_result = scan_result + skip_gain[:, None] * values
    return scan_result.reshape(gate_pre.shape) * jax.nn.silu(gate_pre)


def project(left_operand, right_operand):
    return jnp.einsum(
        "ofp,pv->ofv", left_operand, right_operand, preferred_element_type=jnp.float32
    )


def project_back(left_operand, right_operand):
    return jnp.einsum(
        "igh,rh->igr", left_operand, right_operand, preferred_element_type=jnp.float32
    )


def outer_sum(left_operand, right_operand):
    return jnp.einsum(
        "vzq,vza->qa", left_operand, right_operand, preferred_element_type=jnp.float32
    )


def add_tree(left_operand, right_operand):
    return jax.tree.map(jnp.add, left_operand, right_operand)


def per_device(
    inputs,
    segment,
    cotangent,
    norm_gain,
    weight_z,
    weight_x,
    weight_bc,
    weight_dt,
    conv_weight_x,
    conv_bias_x,
    conv_weight_bc,
    conv_bias_bc,
    step_bias,
    decay_log,
    skip_gain,
    gate_gain,
    weight_out,
):
    model_width = weight_z.shape[0]
    share_width = inputs.shape[2]
    share_start = lax.axis_index("tensor") * share_width
    gain_share = lax.dynamic_slice_in_dim(norm_gain, share_start, share_width, 0)
    bc_share = lax.dynamic_slice_in_dim(weight_bc, share_start, share_width, 0)
    params = (
        conv_weight_x,
        conv_bias_x,
        conv_weight_bc,
        conv_bias_bc,
        step_bias,
        decay_log,
        skip_gain,
    )
    big_grads = None
    small_grads = None
    rounds = inputs.shape[0] // SEQ_MB
    outputs = []
    input_grads = []
    for batch_step in range(rounds):
        row_start = batch_step * SEQ_MB
        local_in = inputs[row_start : row_start + SEQ_MB]
        local_seg = segment[row_start : row_start + SEQ_MB]
        local_cot = cotangent[row_start : row_start + SEQ_MB]
        whole_in, cotangent_entire = (
            lax.all_gather(local_in, "tensor", axis=2, tiled=True),
            lax.all_gather(local_cot, "tensor", axis=2, tiled=True),
        )
        residual = whole_in.astype(jnp.float32)
        scale_in = lax.rsqrt(jnp.mean(residual * residual, axis=-1, keepdims=True) + eps)
        normed = (residual * scale_in * norm_gain).astype(jnp.bfloat16)
        gate_pre = project(normed, weight_z)
        value_pre = project(normed, weight_x)
        bc_pre = project(normed, weight_bc)
        delta_pre = project(normed, weight_dt)

        def local_mixer(gate_in, value_in, bc_in, delta_in, param_set):
            return mixer(gate_in, value_in, bc_in, delta_in, param_set, local_seg)

        gated_out, pullback = jax.vjp(local_mixer, gate_pre, value_pre, bc_pre, delta_pre, params)
        d_mixed = project_back(cotangent_entire, weight_out)
        squares, gate_dot = lax.psum(
            (
                jnp.sum(gated_out * gated_out, axis=-1),
                jnp.sum(d_mixed * gate_gain * gated_out, axis=-1),
            ),
            "tensor",
        )
        scale_gate = lax.rsqrt(squares / INNER + eps)[..., None]
        mixer_output = (gated_out * scale_gate * gate_gain).astype(jnp.bfloat16)
        partial_value = project(mixer_output, weight_out)
        summed = lax.psum_scatter(partial_value, "tensor", scatter_dimension=2, tiled=True)
        outputs.append((local_in.astype(jnp.float32) + summed).astype(jnp.bfloat16))
        grad_out = jnp.einsum(
            "mka,mkg->ag", mixer_output, cotangent_entire, preferred_element_type=jnp.float32
        )
        grad_gate_gain = jnp.sum(d_mixed * gated_out * scale_gate, axis=(0, 1))
        d_gated = (
            scale_gate * gate_gain * d_mixed
            - gated_out * scale_gate**3 * (gate_dot / INNER)[..., None]
        )
        d_gate, d_value, d_bc, d_delta, d_params = pullback(d_gated)
        d_bc, d_conv_weight_bc, d_conv_bias_bc = lax.psum(
            (d_bc, d_params[2], d_params[3]), "tensor"
        )
        low_gate = d_gate.astype(jnp.bfloat16)
        low_value = d_value.astype(jnp.bfloat16)
        low_bc = d_bc.astype(jnp.bfloat16)
        low_delta = d_delta.astype(jnp.bfloat16)
        grad_z = outer_sum(normed, low_gate)
        grad_x = outer_sum(normed, low_value)
        grad_bc = outer_sum(normed, low_bc)
        grad_dt = outer_sum(normed, low_delta)
        d_normed = (
            project_back(low_gate, weight_z)
            + project_back(low_value, weight_x)
            + project_back(low_delta, weight_dt)
        )
        bc_term = project_back(low_bc, bc_share)
        shared_input = lax.dynamic_slice_in_dim(residual, share_start, share_width, 2)
        d_share = lax.psum_scatter(d_normed, "tensor", scatter_dimension=2, tiled=True) + bc_term
        norm_dot = lax.psum(jnp.sum(d_share * gain_share * shared_input, axis=-1), "tensor")
        grad_norm_gain = jnp.sum(d_share * shared_input * scale_in, axis=(0, 1))
        input_grads.append(
            local_cot.astype(jnp.float32)
            + scale_in * gain_share * d_share
            - shared_input * scale_in**3 * (norm_dot / model_width)[..., None]
        )
        big_now = (grad_z, grad_x, grad_bc, grad_dt, grad_out)
        small_now = (
            grad_norm_gain,
            d_params[0],
            d_params[1],
            d_conv_weight_bc,
            d_conv_bias_bc,
            d_params[4],
            d_params[5],
            d_params[6],
            grad_gate_gain,
        )
        big_grads = big_now if big_grads is None else add_tree(big_grads, big_now)
        small_grads = small_now if small_grads is None else add_tree(small_grads, small_now)
    output = jnp.concatenate(outputs, axis=0)
    input_grad = jnp.concatenate(input_grads, axis=0)
    big_grads = (
        lax.psum_scatter(big_grads[0], "dp", scatter_dimension=0, tiled=True),
        lax.psum_scatter(big_grads[1], "dp", scatter_dimension=0, tiled=True),
        lax.psum_scatter(big_grads[2], "dp", scatter_dimension=0, tiled=True),
        lax.psum_scatter(big_grads[3], "dp", scatter_dimension=0, tiled=True),
        lax.psum_scatter(big_grads[4], "dp", scatter_dimension=1, tiled=True),
    )
    small_grads = lax.psum(small_grads, "dp")
    return (
        output,
        input_grad,
        small_grads[0],
        big_grads[0],
        big_grads[1],
        big_grads[2],
        big_grads[3],
        small_grads[1],
        small_grads[2],
        small_grads[3],
        small_grads[4],
        small_grads[5],
        small_grads[6],
        small_grads[7],
        small_grads[8],
        big_grads[4],
    )


def solution(mesh):
    return jax.shard_map(
        per_device,
        mesh=mesh,
        in_specs=(
            P("dp", None, "tensor"),
            P("dp", None),
            P("dp", None, "tensor"),
            P(),
            P(None, "tensor"),
            P(None, "tensor"),
            P(),
            P(None, "tensor"),
            P(None, "tensor"),
            P("tensor"),
            P(),
            P(),
            P("tensor"),
            P("tensor"),
            P("tensor"),
            P("tensor"),
            P("tensor", None),
        ),
        out_specs=(
            P("dp", None, "tensor"),
            P("dp", None, "tensor"),
            P("tensor"),
            P("dp", "tensor"),
            P("dp", "tensor"),
            P("dp", None),
            P("dp", "tensor"),
            P(None, "tensor"),
            P("tensor"),
            P(),
            P(),
            P("tensor"),
            P("tensor"),
            P("tensor"),
            P("tensor"),
            P("tensor", "dp"),
        ),
        check_vma=False,
    )
```

profile of v0, /device:TPU:0, one launch (start us, length us, event | category | flops | bytes accessed | tf_op | source)
XLA Modules:
  0.0 1255.8 jit_solution(11214322786182025757)
XLA Ops:
  14.4 44.7 %all-gather.5.cloned.1.call-done = bf16[1,1024,1024]{2,1,0:T(8,128)(2,1)} async-done(((bf16[1,1024,256]{2,1,0:T(8,128)(2,1)}), bf16[1,1024,1024]{2,1,0:T(8,128)(2,1)}) %all-gather.5.cloned.1.call-update) | async-done | bytes 2097168 | tf_op jit(solution)/shard_map/all_gather | solution.py:159
  62.0 43.8 %all-gather.7.cloned.1.call-done = bf16[1,1024,1024]{2,1,0:T(8,128)(2,1)} async-done(((bf16[1,1024,256]{2,1,0:T(8,128)(2,1)}), bf16[1,1024,1024]{2,1,0:T(8,128)(2,1)}) %all-gather.7.cloned.1.call-update) | async-done | bytes 2097168 | tf_op jit(solution)/shard_map/all_gather | solution.py:159
  123.0 5.0 fusion.299
  140.0 58.6 %while.91 = (s32[]{:T(128)}, f32[1,8,128,64]{2,3,1,0:T(8,128)}, s32[1]{0:T(128)}, f32[4,1,256,8,64]{2,4,3,1,0:T(8,128)}, f32[4,1,8,128,64]{3,4,2,1,0:T(8,128)}, ...) while((s32[]{:T(128)}, f32[1,8,128,64]{2,3,1,0:T(8,128)}, ...), condition=%wide.region_12.14_spmd.clone, body=%wide.region_9.13_spmd.clone.sunk | while | flops 909716480 | bytes 14458493 | solution.py:71
  220.5 58.8 %while.90 = (s32[]{:T(128)}, f32[1,8,128,64]{2,3,1,0:T(8,128)}, s32[1]{0:T(128)}, f32[4,1,256,8,64]{2,4,3,1,0:T(8,128)}, f32[4,1,8,128,64]{3,4,2,1,0:T(8,128)}, ...) while((s32[]{:T(128)}, f32[1,8,128,64]{2,3,1,0:T(8,128)}, ...), condition=%wide.region_4.6_spmd.clone, body=%wide.region_1.5_spmd.clone.sunk | while | flops 909716480 | bytes 14458309 | solution.py:71
  296.8 9.4 all-reduce.58
  310.8 7.2 multiply_reduce_fusion.11
  318.0 9.8 all-reduce.57
  328.0 8.7 fusion.281
  357.4 126.8 %while.92 = (s32[]{:T(128)}, f32[1,8,128,64]{2,3,1,0:T(8,128)S(1)}, f32[4,1,256,8,64]{2,4,3,1,0:T(8,128)}, f32[4,1,256,8]{2,3,1,0:T(8,128)}, f32[4,1,256,8]{2,3,...) while((s32[]{:T(128)}, f32[1,8,128,64]{2,3,1,0:T(8,128)S(1)}, ...), condition=%wide.region_31.33_spmd.clone, body=%wide.region_18.32_spmd.clone.sunk | while | flops 2126752768 | bytes 21947920 | solution.py:71
  496.9 128.2 %while.93 = (s32[]{:T(128)}, f32[1,8,128,64]{2,3,1,0:T(8,128)S(1)}, f32[4,1,256,8,64]{2,4,3,1,0:T(8,128)}, f32[4,1,256,8]{2,3,1,0:T(8,128)}, f32[4,1,256,8]{2,3,...) while((s32[]{:T(128)}, f32[1,8,128,64]{2,3,1,0:T(8,128)S(1)}, ...), condition=%wide.region_51.53_spmd.clone, body=%wide.region_38.52_spmd.clone.sunk | while | flops 2126752768 | bytes 20604208 | solution.py:71
  633.9 8.2 multiply_reduce_fusion.19
  650.9 6.6 multiply_reduce_fusion.15
  698.8 130.9 %all-reduce.60 = (bf16[1,1024,256]{2,1,0:T(8,128)(2,1)}, bf16[1,1024,256]{2,1,0:T(8,128)(2,1)}) all-reduce(f32[1,1024,256]{2,1,0:T(8,128)} %get-tuple-element.1710, f32[1,1024,256]{2,1,0:T(8,128)} %get-tuple-element.1709), channel_id=1, replica_groups=mesh['dp'=8,'tensor'=4] {'tensor'}, use_global_device_ids=true, to_apply=%region_53.55 | all-reduce | flops 524288 | bytes 3145728 | tf_op jit(solution)/shard_map/psum | solution.py:196
  863.2 15.0 %reduce-scatter.14.cloned.1.call-done = f32[1,1024,256]{2,1,0:T(8,128)} async-done(((f32[1,1024,1024]{2,1,0:T(8,128)}), f32[1,1024,256]{2,1,0:T(8,128)}) %reduce-scatter.14.cloned.1.call-update) | async-done | bytes 1048592 | tf_op jit(solution)/shard_map/reduce_scatter | solution.py:214
  881.1 18.4 %all-reduce.55 = (f32[1,1024]{1,0:T(1,128)S(1)}, f32[1,1024]{1,0:T(1,128)S(1)}, f32[4,256]{1,0:T(4,128)S(1)}, f32[256]{0:T(256)S(1)}) all-reduce(f32[1,1024]{1,0:T(1,128)S(1)} %bitcast.1481, f32[1,1024]{1,0:T(1,128)S(1)} %bitcast.1480, f32[4,256]{1,0:T(4,128)S(1)} %add_add_fusion.1, ...), channel_id=1, replica_groups=mesh['dp'=8,'tensor'=4] {'tensor'}, use_global_device_ids=true, to_apply=%region_55.57 | all-reduce | flops 3328 | bytes 26624 | tf_op jit(solution)/shard_map/psum | solution.py:215
  899.5 24.6 %all-reduce.54 = (f32[256]{0:T(256)}, f32[4,512]{1,0:T(4,128)}, f32[512]{0:T(512)}, f32[4,256]{1,0:T(4,128)}, f32[256]{0:T(256)}, /*index=5*/f32[8]{0:T(128)}, f32[8]{0:T(128)}, f32[8]{0:T(128)}, f32[512]{0:T(512)}) all-reduce(f32[256]{0:T(256)S(1)} %add.531, ...), channel_id=1, replica_groups=mesh['dp'=8,'tensor'=4] {'dp'}, use_global_device_ids=true, to_apply=%region_58.60 | all-reduce | flops 4632 | bytes 37056 | tf_op jit(solution)/shard_map/psum | solution.py:245
  924.1 34.1 %reduce-scatter.12.cloned.1.call-done = f32[1,1024,256]{2,1,0:T(8,128)} async-done(((f32[1,1024,1024]{2,1,0:T(8,128)}), f32[1,1024,256]{2,1,0:T(8,128)}) %reduce-scatter.12.cloned.1.call-update) | async-done | bytes 1048592 | tf_op jit(solution)/shard_map/reduce_scatter | solution.py:185
  958.2 79.6 %reduce-scatter.10.cloned.1.call-done = f32[1,1024,256]{2,1,0:T(8,128)} async-done(((f32[1,1024,1024]{2,1,0:T(8,128)}), f32[1,1024,256]{2,1,0:T(8,128)}) %reduce-scatter.10.cloned.1.call-update) | async-done | bytes 1048592 | tf_op jit(solution)/shard_map/reduce_scatter | solution.py:185
  1045.4 27.8 %reduce-scatter.24.cloned.1.call-done = f32[128,8]{0,1:T(8,128)} async-done(((f32[1024,8]{0,1:T(8,128)}), f32[128,8]{0,1:T(8,128)}) %reduce-scatter.24.cloned.1.call-update) | async-done | bytes 4112 | tf_op jit(solution)/shard_map/reduce_scatter | solution.py:242
  1073.1 40.0 %reduce-scatter.22.cloned.1.call-done = f32[128,256]{1,0:T(8,128)} async-done(((f32[1024,256]{1,0:T(8,128)}), f32[128,256]{1,0:T(8,128)}) %reduce-scatter.22.cloned.1.call-update) | async-done | bytes 131088 | tf_op jit(solution)/shard_map/reduce_scatter | solution.py:241
  1113.2 45.5 %reduce-scatter.26.cloned.1.call-done = f32[512,128]{1,0:T(8,128)} async-done(((f32[512,1024]{1,0:T(8,128)}), f32[512,128]{1,0:T(8,128)}) %reduce-scatter.26.cloned.1.call-update) | async-done | bytes 262160 | tf_op jit(solution)/shard_map/reduce_scatter | solution.py:243
  1158.6 45.0 %reduce-scatter.20.cloned.1.call-done = f32[128,512]{1,0:T(8,128)} async-done(((f32[1024,512]{1,0:T(8,128)}), f32[128,512]{1,0:T(8,128)}) %reduce-scatter.20.cloned.1.call-update) | async-done | bytes 262160 | tf_op jit(solution)/shard_map/reduce_scatter | solution.py:240
  1203.6 45.5 %reduce-scatter.18.cloned.1.call-done = f32[128,512]{1,0:T(8,128)} async-done(((f32[1024,512]{1,0:T(8,128)}), f32[128,512]{1,0:T(8,128)}) %reduce-scatter.18.cloned.1.call-update) | async-done | bytes 262160 | tf_op jit(solution)/shard_map/reduce_scatter | solution.py:239
  (1177 shorter events, 566.2 us)
Async XLA Ops:
  7.2 280.7 %copy-start = (bf16[1024,512]{1,0:T(8,128)(2,1)S(1)}, bf16[1024,512]{1,0:T(8,128)(2,1)}, u32[]{:S(2)}) copy-start(bf16[1024,512]{1,0:T(8,128)(2,1)} %param.30) | copy-start | bytes 3145732
  7.2 51.9 %all-gather.5.cloned.1.call-start = ((), (), s32[]{:S(2)}) async-start(), calls=%async_computation.9 | async-start | bytes 2621440 | tf_op jit(solution)/shard_map/all_gather | solution.py:159
  9.7 96.1 %all-gather.7.cloned.1.call-start = ((), (), s32[]{:S(2)}) async-start(), calls=%async_computation.11 | async-start | bytes 2621440 | tf_op jit(solution)/shard_map/all_gather | solution.py:159
  10.4 296.0 %all-gather.11.cloned.1.call-start = ((), (), s32[]{:S(2)}) async-start(), calls=%async_computation.15 | async-start | bytes 2621440 | tf_op jit(solution)/shard_map/all_gather | solution.py:160
  11.6 299.3 %all-gather.9.cloned.1.call-start = ((), (), s32[]{:S(2)}) async-start(), calls=%async_computation.13 | async-start | bytes 2621440 | tf_op jit(solution)/shard_map/all_gather | solution.py:160
  12.1 849.4 %reduce-scatter.16.cloned.1.call-start = ((), (), s32[]{:S(2)}) async-start(), calls=%async_computation.16 | async-start | bytes 5242880 | tf_op jit(solution)/shard_map/reduce_scatter | solution.py:214
  13.5 109.5 %copy-start.113 = (f32[1,512]{1,0:T(1,128)}, f32[1,512]{1,0:T(1,128)S(1)}, u32[]{:S(2)}) copy-start(f32[1,512]{1,0:T(1,128)S(1)} %get-tuple-element.1669) | copy-start | bytes 6148
  13.5 109.5 %copy-start.115 = (f32[1,512]{1,0:T(1,128)}, f32[1,512]{1,0:T(1,128)S(1)}, u32[]{:S(2)}) copy-start(f32[1,512]{1,0:T(1,128)S(1)} %get-tuple-element.1670) | copy-start | bytes 6148
  13.5 101.8 %copy-start.138 = (f32[8]{0:T(128)}, f32[8]{0:T(128)S(1)}, u32[]{:S(2)}) copy-start(f32[8]{0:T(128)S(1)} %exp.270) | copy-start | bytes 100
  14.3 108.6 %copy-start.79 = (f32[1,1024]{1,0:T(1,128)}, f32[1,1024]{1,0:T(1,128)S(1)}, u32[]{:S(2)}) copy-start(f32[1,1024]{1,0:T(1,128)S(1)} %get-tuple-element.1693) | copy-start | bytes 12292
  14.4 108.6 %copy-start.81 = (f32[1,1024]{1,0:T(1,128)}, f32[1,1024]{1,0:T(1,128)S(1)}, u32[]{:S(2)}) copy-start(f32[1,1024]{1,0:T(1,128)S(1)} %get-tuple-element.1694) | copy-start | bytes 12292
  14.4 108.6 %copy-start.83 = (f32[1,1024]{1,0:T(1,128)}, f32[1,1024]{1,0:T(1,128)S(1)}, u32[]{:S(2)}) copy-start(f32[1,1024]{1,0:T(1,128)S(1)} %get-tuple-element.1695) | copy-start | bytes 12292
  14.4 108.6 %copy-start.85 = (f32[1,1024]{1,0:T(1,128)}, f32[1,1024]{1,0:T(1,128)S(1)}, u32[]{:S(2)}) copy-start(f32[1,1024]{1,0:T(1,128)S(1)} %get-tuple-element.1719) | copy-start | bytes 12292
  14.4 108.6 %copy-start.87 = (f32[1,1024]{1,0:T(1,128)}, f32[1,1024]{1,0:T(1,128)S(1)}, u32[]{:S(2)}) copy-start(f32[1,1024]{1,0:T(1,128)S(1)} %get-tuple-element.1720) | copy-start | bytes 12292
  14.4 108.6 %copy-start.89 = (f32[1,1024]{1,0:T(1,128)}, f32[1,1024]{1,0:T(1,128)S(1)}, u32[]{:S(2)}) copy-start(f32[1,1024]{1,0:T(1,128)S(1)} %get-tuple-element.1721) | copy-start | bytes 12292
  128.0 208.7 %copy-start.1 = (f32[1,1024,512]{2,1,0:T(8,128)}, f32[1,1024,512]{2,1,0:T(8,128)S(1)}, u32[]{:S(2)}) copy-start(f32[1,1024,512]{2,1,0:T(8,128)S(1)} %get-tuple-element.1666) | copy-start | bytes 6291460
  668.0 210.1 %reduce-scatter.14.cloned.1.call-start = ((), (), s32[]{:S(2)}) async-start(), calls=%async_computation.14 | async-start | bytes 5242880 | tf_op jit(solution)/shard_map/reduce_scatter | solution.py:214
  675.9 282.3 %reduce-scatter.12.cloned.1.call-start = ((), (), s32[]{:S(2)}) async-start(), calls=%async_computation.12 | async-start | bytes 5242880 | tf_op jit(solution)/shard_map/reduce_scatter | solution.py:185
  681.9 355.9 %reduce-scatter.10.cloned.1.call-start = ((), (), s32[]{:S(2)}) async-start(), calls=%async_computation.10 | async-start | bytes 5242880 | tf_op jit(solution)/shard_map/reduce_scatter | solution.py:185
  688.0 385.1 %reduce-scatter.24.cloned.1.call-start = ((), (), s32[]{:S(2)}) async-start(), calls=%async_computation.20 | async-start | bytes 36864 | tf_op jit(solution)/shard_map/reduce_scatter | solution.py:242
  833.1 280.1 %reduce-scatter.22.cloned.1.call-start = ((), (), s32[]{:S(2)}) async-start(), calls=%async_computation.19 | async-start | bytes 1179648 | tf_op jit(solution)/shard_map/reduce_scatter | solution.py:241
  836.3 322.4 %reduce-scatter.26.cloned.1.call-start = ((), (), s32[]{:S(2)}) async-start(), calls=%async_computation.21 | async-start | bytes 2359296 | tf_op jit(solution)/shard_map/reduce_scatter | solution.py:243
  842.8 360.8 %reduce-scatter.20.cloned.1.call-start = ((), (), s32[]{:S(2)}) async-start(), calls=%async_computation.18 | async-start | bytes 2359296 | tf_op jit(solution)/shard_map/reduce_scatter | solution.py:240
  848.8 400.3 %reduce-scatter.18.cloned.1.call-start = ((), (), s32[]{:S(2)}) async-start(), calls=%async_computation.17 | async-start | bytes 2359296 | tf_op jit(solution)/shard_map/reduce_scatter | solution.py:239
  (240 other events, 1410.3 us)
Sparse Core Ops, SparseCore 0:
  10.2 48.9 all-gather.4
  61.3 44.4 all-gather.6
  107.4 44.4 all-gather.10
  153.3 44.4 all-gather.8
  668.1 112.7 reduce-scatter.15
  783.1 94.9 reduce-scatter.13
  880.4 77.7 reduce-scatter.11
  960.6 77.1 reduce-scatter.9
  1041.4 31.7 reduce-scatter.23
  1077.1 36.0 reduce-scatter.21
  1117.4 41.2 reduce-scatter.25
  1162.3 41.2 reduce-scatter.19
  1207.8 41.2 reduce-scatter.17
where the time goes:
time: 1270 us; the launch traced here: 1260 us
  waiting for transfers between devices  422 us (33%)
  matrix products  258 us (20%)
  blocking collectives  193 us (15%)
  local copies, waits for them, and re-layouts  173 us (14%)
  other arithmetic  169 us (13%)
  loops' own time  24.3 us (2%)
  between operations  15.6 us (1%)
    psum x1, blocking collectives, per_device(): lax.psum((d_bc, d_params[2], d_params[3]), 'tensor')  131 us
    reduce_scatter x2, waiting for transfers between devices, per_device(): lax.psum_scatter(partial_value, 'tensor', scatter_dimension=2, tiled=True)  114 us
    dot_general x24, matrix products, advance(): jnp.einsum('stuh,suhp->sthp', mixing, value_blk, precision=lax.Precision....  91.5 us
    all_gather x2, waiting for transfers between devices, per_device(): lax.all_gather(local_in, 'tensor', axis=2, tiled=True)  88.5 us
    reduce_scatter x1, waiting for transfers between devices, per_device(): lax.psum_scatter(big_grads[4], 'dp', scatter_dimension=1, tiled=True)  45.5 us
    reduce_scatter x1, waiting for transfers between devices, per_device(): lax.psum_scatter(big_grads[0], 'dp', scatter_dimension=0, tiled=True)  45.5 us
    reduce_scatter x1, waiting for transfers between devices, per_device(): lax.psum_scatter(big_grads[1], 'dp', scatter_dimension=0, tiled=True)  45 us
    reduce_scatter x1, waiting for transfers between devices, per_device(): lax.psum_scatter(big_grads[2], 'dp', scatter_dimension=0, tiled=True)  40 us
  transfers between devices with their start and end apart: 13, of which 10 were waited for; matrix products, arithmetic and copies ran while one was open for 20% of the time, Pallas kernels for 0%

commit v1 on v0

--- a/solution.py
+++ b/solution.py
@@ -7,6 +7,24 @@
 SEQ_MB = 1
 INNER = 2048
 eps = 1e-05
+
+
+def gather_around(array, axis, dim):
+    ways, here, step = (lax.axis_size(axis), lax.axis_index(axis), array.shape[dim])
+    lengths = [n * ways if d == dim else n for d, n in enumerate(array.shape)]
+    full = lax.dynamic_update_slice_in_dim(
+        jnp.zeros(lengths, array.dtype), array, here * step, axis=dim
+    )
+    going_up = going_down = array
+    for far in range(1, ways // 2 + 1):
+        going_up = lax.ppermute(going_up, axis, [(d, (d + 1) % ways) for d in range(ways)])
+        full = lax.dynamic_update_slice_in_dim(full, going_up, (here - far) % ways * step, axis=dim)
+        if 2 * far < ways:
+            going_down = lax.ppermute(going_down, axis, [(d, (d - 1) % ways) for d in range(ways)])
+            full = lax.dynamic_update_slice_in_dim(
+                full, going_down, (here + far) % ways * step, axis=dim
+            )
+    return full
 
 
 def causal_conv(values, weights, biases, segment):
@@ -156,7 +174,7 @@
         local_seg = segment[row_start : row_start + SEQ_MB]
         local_cot = cotangent[row_start : row_start + SEQ_MB]
         whole_in, cotangent_entire = (
-            lax.all_gather(local_in, "tensor", axis=2, tiled=True),
+            gather_around(local_in, "tensor", 2),
             lax.all_gather(local_cot, "tensor", axis=2, tiled=True),
         )
         residual = whole_in.astype(jnp.float32)

time: 1270 us -> 1160 us (0.913)
  waiting for transfers between devices: 422 us -> 247 us
  starting transfers between devices: 1.11 us -> 43.5 us
  local copies, waits for them, and re-layouts: 173 us -> 201 us
    reduce_scatter x2, waiting for transfers between devices: 114 us -> 0.04 us  [per_device(): lax.psum_scatter(partial_value, 'tensor', scatter_dimension=2, tiled=True)]
    all_gather x2 -> x0, waiting for transfers between devices: 88.5 us -> none  [per_device(): lax.all_gather(local_in, 'tensor', axis=2, tiled=True)]
    ppermute x0 -> x6, waiting for transfers between devices: none -> 54.4 us  [the longest x4 50.9 us: gather_around(): lax.ppermute(going_up, axis, [(d, (d + 1) % ways) for d in range(ways)])]
    ppermute x0 -> x6, starting transfers between devices: none -> 42.7 us  [the longest x4 36.8 us: gather_around(): lax.ppermute(going_up, axis, [(d, (d + 1) % ways) for d in range(ways)])]
    reduce_scatter x1, waiting for transfers between devices: 27.8 us -> 0.01 us  [per_device(): lax.psum_scatter(big_grads[3], 'dp', scatter_dimension=0, tiled=True)]
    reduce_scatter x2, waiting for transfers between devices: 15 us -> 29.1 us  [per_device(): lax.psum_scatter(d_normed, 'tensor', scatter_dimension=2, tiled=True)]
    unnamed x250 -> x258, local copies, waits for them, and re-layouts: 28.7 us -> 26.3 us
  transfers between devices with their start and end apart: 13 -> 17, of which waited for: 10 -> 10; matrix products, arithmetic and copies ran while one was open for 20% -> 53% of each run, Pallas kernels for 0% -> 0%
where the time goes in v1:
time: 1160 us
  matrix products  249 us (21%)
  waiting for transfers between devices  247 us (21%)
  local copies, waits for them, and re-layouts  201 us (17%)
  blocking collectives  195 us (17%)
  other arithmetic  180 us (16%)
  starting transfers between devices  43.5 us (4%)
  loops' own time  24.1 us (2%)
  between operations  16 us (1%)
    psum x1, blocking collectives, per_device(): lax.psum((d_bc, d_params[2], d_params[3]), 'tensor')  125 us
    dot_general x24, matrix products, advance(): jnp.einsum('stuh,suhp->sthp', mixing, value_blk, precision=lax.Precision....  90.6 us
    ppermute x4, waiting for transfers between devices, gather_around(): lax.ppermute(going_up, axis, [(d, (d + 1) % ways) for d in range(ways)])  50.9 us
    another operation x57, other arithmetic  49.8 us
    reduce_scatter x1, waiting for transfers between devices, per_device(): lax.psum_scatter(big_grads[0], 'dp', scatter_dimension=0, tiled=True)  45.5 us
    reduce_scatter x1, waiting for transfers between devices, per_device(): lax.psum_scatter(big_grads[4], 'dp', scatter_dimension=1, tiled=True)  45.5 us
    reduce_scatter x1, waiting for transfers between devices, per_device(): lax.psum_scatter(big_grads[1], 'dp', scatter_dimension=0, tiled=True)  45 us
    ppermute x4, starting transfers between devices, gather_around(): lax.ppermute(going_up, axis, [(d, (d + 1) % ways) for d in range(ways)])  36.8 us
  transfers between devices with their start and end apart: 17, of which 10 were waited for; matrix products, arithmetic and copies ran while one was open for 53% of the time, Pallas kernels for 0%

profile of v1, /device:TPU:0, one launch (start us, length us, event | category | flops | bytes accessed | tf_op | source)
XLA Modules:
  0.0 1156.1 jit_solution(3807847826851456578)
XLA Ops:
  25.3 10.2 collective-permute-done.3
  35.6 20.0 %collective-permute-start.5 = (bf16[1,1024,256]{2,1,0:T(8,128)(2,1)}, bf16[1,1024,256]{2,1,0:T(8,128)(2,1)}, u32[]{:S(2)}, u32[]{:S(2)}) collective-permute-start(bf16[1,1024,256]{2,1,0:T(8,128)(2,1)} %collective-permute-done.3), channel_id=1, source_target_pairs={{0,1},{1,2},{2,3},{3,0},{4,5},{5,6},{6,7},{7,4},{8,9},{9,10},{10,1... | collective-permute-start | bytes 1572872 | tf_op jit(solution)/shard_map/ppermute | solution.py:20
  55.9 18.9 %collective-permute-done = bf16[1,1024,256]{2,1,0:T(8,128)(2,1)} collective-permute-done((bf16[1,1024,256]{2,1,0:T(8,128)(2,1)}, bf16[1,1024,256]{2,1,0:T(8,128)(2,1)}, u32[]{:S(2)}, u32[]{:S(2)}) %collective-permute-start) | collective-permute-done | bytes 524320 | tf_op jit(solution)/shard_map/ppermute | solution.py:20
  74.8 13.7 %collective-permute-start.2 = (bf16[1,1024,256]{2,1,0:T(8,128)(2,1)}, bf16[1,1024,256]{2,1,0:T(8,128)(2,1)S(1)}, u32[]{:S(2)}, u32[]{:S(2)}) collective-permute-start(bf16[1,1024,256]{2,1,0:T(8,128)(2,1)} %collective-permute-done), channel_id=1, source_target_pairs={{0,1},{1,2},{2,3},{3,0},{4,5},{5,6},{6,7},{7,4},{8,9},{9,10},{10,1... | collective-permute-start | bytes 1572872 | tf_op jit(solution)/shard_map/ppermute | solution.py:20
  98.2 10.8 collective-permute-done.5
  113.7 10.9 collective-permute-done.2
  159.0 74.6 %while.91 = (s32[]{:T(128)}, f32[1,8,128,64]{2,3,1,0:T(8,128)}, s32[1]{0:T(128)}, f32[4,1,256,8,64]{2,4,3,1,0:T(8,128)}, f32[4,1,8,128,64]{3,4,2,1,0:T(8,128)}, ...) while((s32[]{:T(128)}, f32[1,8,128,64]{2,3,1,0:T(8,128)}, ...), condition=%wide.region_12.14_spmd.clone, body=%wide.region_9.13_spmd.clone.sunk | while | flops 909716480 | bytes 14458309 | solution.py:89
  247.0 50.1 %while.90 = (s32[]{:T(128)}, f32[1,8,128,64]{2,3,1,0:T(8,128)S(1)}, s32[1]{0:T(128)}, f32[4,1,256,8,64]{2,4,3,1,0:T(8,128)}, f32[4,1,8,128,64]{3,4,2,1,0:T(8,128...) while((s32[]{:T(128)}, f32[1,8,128,64]{2,3,1,0:T(8,128)S(1)}, ...), condition=%wide.region_4.6_spmd.clone, body=%wide.region_1.5_spmd.clone.sunk | while | flops 909716480 | bytes 14458309 | solution.py:89
  323.3 18.3 %all-reduce.58 = (f32[1,1024]{1,0:T(1,128)S(1)}, f32[1,1024]{1,0:T(1,128)S(1)}) all-reduce(f32[1,1024]{1,0:T(1,128)S(1)} %bitcast.1498, f32[1,1024]{1,0:T(1,128)S(1)} %bitcast.1497), channel_id=1, replica_groups=mesh['dp'=8,'tensor'=4] {'tensor'}, use_global_device_ids=true, to_apply=%region_14.16 | all-reduce | flops 2048 | bytes 16384 | tf_op jit(solution)/shard_map/psum | solution.py:193
  347.2 5.1 convolution_bitcast_fusion.13
  357.2 7.2 multiply_reduce_fusion.11
  364.4 11.9 %all-reduce.57 = (f32[1,1024]{1,0:T(1,128)S(1)}, f32[1,1024]{1,0:T(1,128)S(1)}) all-reduce(f32[1,1024]{1,0:T(1,128)S(1)} %bitcast.1480, f32[1,1024]{1,0:T(1,128)S(1)} %bitcast.1479), channel_id=1, replica_groups=mesh['dp'=8,'tensor'=4] {'tensor'}, use_global_device_ids=true, to_apply=%region_37.39 | all-reduce | flops 2048 | bytes 16384 | tf_op jit(solution)/shard_map/psum | solution.py:193
  376.4 8.5 fusion.281
  397.5 132.8 %while.92 = (s32[]{:T(128)}, f32[1,8,128,64]{2,3,1,0:T(8,128)S(1)}, f32[4,1,256,8,64]{2,4,3,1,0:T(8,128)}, f32[4,1,256,8]{2,3,1,0:T(8,128)}, f32[4,1,256,8]{2,3,...) while((s32[]{:T(128)}, f32[1,8,128,64]{2,3,1,0:T(8,128)S(1)}, ...), condition=%wide.region_31.33_spmd.clone, body=%wide.region_18.32_spmd.clone.sunk | while | flops 2126752768 | bytes 22006084 | solution.py:89
  543.1 140.3 %while.93 = (s32[]{:T(128)}, f32[1,8,128,64]{2,3,1,0:T(8,128)S(1)}, f32[4,1,256,8,64]{2,4,3,1,0:T(8,128)}, f32[4,1,256,8]{2,3,1,0:T(8,128)}, f32[4,1,256,8]{2,3,...) while((s32[]{:T(128)}, f32[1,8,128,64]{2,3,1,0:T(8,128)S(1)}, ...), condition=%wide.region_51.53_spmd.clone, body=%wide.region_38.52_spmd.clone.sunk | while | flops 2126752768 | bytes 21448676 | solution.py:89
  700.6 6.3 multiply_reduce_fusion.19
  746.9 124.7 %all-reduce.60 = (bf16[1,1024,256]{2,1,0:T(8,128)(2,1)}, bf16[1,1024,256]{2,1,0:T(8,128)(2,1)}) all-reduce(f32[1,1024,256]{2,1,0:T(8,128)} %get-tuple-element.1711, f32[1,1024,256]{2,1,0:T(8,128)} %get-tuple-element.1710), channel_id=1, replica_groups=mesh['dp'=8,'tensor'=4] {'tensor'}, use_global_device_ids=true, to_apply=%region_53.55 | all-reduce | flops 524288 | bytes 3145728 | tf_op jit(solution)/shard_map/psum | solution.py:214
  909.5 29.1 %reduce-scatter.14.cloned.1.call-done = f32[1,1024,256]{2,1,0:T(8,128)} async-done(((f32[1,1024,1024]{2,1,0:T(8,128)}), f32[1,1024,256]{2,1,0:T(8,128)}) %reduce-scatter.14.cloned.1.call-update) | async-done | bytes 1048592 | tf_op jit(solution)/shard_map/reduce_scatter | solution.py:232
  941.6 17.2 %all-reduce.55 = (f32[1,1024]{1,0:T(1,128)S(1)}, f32[1,1024]{1,0:T(1,128)S(1)}, f32[4,256]{1,0:T(4,128)S(1)}, f32[256]{0:T(256)S(1)}) all-reduce(f32[1,1024]{1,0:T(1,128)S(1)} %bitcast.1478, f32[1,1024]{1,0:T(1,128)S(1)} %bitcast.1477, f32[4,256]{1,0:T(4,128)S(1)} %add_add_fusion.1, ...), channel_id=1, replica_groups=mesh['dp'=8,'tensor'=4] {'tensor'}, use_global_device_ids=true, to_apply=%region_55.57 | all-reduce | flops 3328 | bytes 26624 | tf_op jit(solution)/shard_map/psum | solution.py:233
  958.9 22.9 %all-reduce.54 = (f32[256]{0:T(256)}, f32[4,512]{1,0:T(4,128)}, f32[512]{0:T(512)}, f32[4,256]{1,0:T(4,128)}, f32[256]{0:T(256)}, /*index=5*/f32[8]{0:T(128)}, f32[8]{0:T(128)}, f32[8]{0:T(128)}, f32[512]{0:T(512)}) all-reduce(f32[256]{0:T(256)S(1)} %add.571, ...), channel_id=1, replica_groups=mesh['dp'=8,'tensor'=4] {'dp'}, use_global_device_ids=true, to_apply=%region_58.60 | all-reduce | flops 4632 | bytes 37056 | tf_op jit(solution)/shard_map/psum | solution.py:263
  985.9 27.5 %reduce-scatter.22.cloned.1.call-done = f32[128,256]{1,0:T(8,128)} async-done(((f32[1024,256]{1,0:T(8,128)}), f32[128,256]{1,0:T(8,128)}) %reduce-scatter.22.cloned.1.call-update) | async-done | bytes 131088 | tf_op jit(solution)/shard_map/reduce_scatter | solution.py:259
  1013.5 45.5 %reduce-scatter.26.cloned.1.call-done = f32[512,128]{1,0:T(8,128)} async-done(((f32[512,1024]{1,0:T(8,128)}), f32[512,128]{1,0:T(8,128)}) %reduce-scatter.26.cloned.1.call-update) | async-done | bytes 262160 | tf_op jit(solution)/shard_map/reduce_scatter | solution.py:261
  1058.9 45.0 %reduce-scatter.20.cloned.1.call-done = f32[128,512]{1,0:T(8,128)} async-done(((f32[1024,512]{1,0:T(8,128)}), f32[128,512]{1,0:T(8,128)}) %reduce-scatter.20.cloned.1.call-update) | async-done | bytes 262160 | tf_op jit(solution)/shard_map/reduce_scatter | solution.py:258
  1103.9 45.5 %reduce-scatter.18.cloned.1.call-done = f32[128,512]{1,0:T(8,128)} async-done(((f32[1024,512]{1,0:T(8,128)}), f32[128,512]{1,0:T(8,128)}) %reduce-scatter.18.cloned.1.call-update) | async-done | bytes 262160 | tf_op jit(solution)/shard_map/reduce_scatter | solution.py:257
  (1216 shorter events, 616.7 us)
Async XLA Ops:
  7.2 307.1 %copy-start = (bf16[1024,512]{1,0:T(8,128)(2,1)S(1)}, bf16[1024,512]{1,0:T(8,128)(2,1)}, u32[]{:S(2)}) copy-start(bf16[1024,512]{1,0:T(8,128)(2,1)} %param.30) | copy-start | bytes 3145732
  7.2 345.2 %all-gather.5.cloned.1.call-start = ((), (), s32[]{:S(2)}) async-start(), calls=%async_computation.13 | async-start | bytes 2621440 | tf_op jit(solution)/shard_map/all_gather | solution.py:178
  9.7 347.6 %all-gather.3.cloned.1.call-start = ((), (), s32[]{:S(2)}) async-start(), calls=%async_computation.11 | async-start | bytes 2621440 | tf_op jit(solution)/shard_map/all_gather | solution.py:178
  12.1 23.5 %collective-permute-start.3 = (bf16[1,1024,256]{2,1,0:T(8,128)(2,1)}, bf16[1,1024,256]{2,1,0:T(8,128)(2,1)}, u32[]{:S(2)}, u32[]{:S(2)}) collective-permute-start(bf16[1,1024,256]{2,1,0:T(8,128)(2,1)} %get-tuple-element.1657), channel_id=1, source_target_pairs={{0,1},{1,2},{2,3},{3,0},{4,5},{5,6},{6,7},{7,4},{8,9},{9,10},{10,1... | collective-permute-start | bytes 1572872 | tf_op jit(solution)/shard_map/ppermute | solution.py:20
  15.2 76.4 %collective-permute-start.4 = (bf16[1,1024,256]{2,1,0:T(8,128)(2,1)}, bf16[1,1024,256]{2,1,0:T(8,128)(2,1)}, u32[]{:S(2)}, u32[]{:S(2)}) collective-permute-start(bf16[1,1024,256]{2,1,0:T(8,128)(2,1)} %get-tuple-element.1657), channel_id=1, source_target_pairs={{0,3},{1,0},{2,1},{3,2},{4,7},{5,4},{6,5},{7,6},{8,11},{9,8},{10,9... | collective-permute-start | bytes 1572872 | tf_op jit(solution)/shard_map/ppermute | solution.py:23
  17.3 57.5 %collective-permute-start = (bf16[1,1024,256]{2,1,0:T(8,128)(2,1)}, bf16[1,1024,256]{2,1,0:T(8,128)(2,1)}, u32[]{:S(2)}, u32[]{:S(2)}) collective-permute-start(bf16[1,1024,256]{2,1,0:T(8,128)(2,1)} %get-tuple-element.1655), channel_id=1, source_target_pairs={{0,1},{1,2},{2,3},{3,0},{4,5},{5,6},{6,7},{7,4},{8,9},{9,10},{10,1... | collective-permute-start | bytes 1572872 | tf_op jit(solution)/shard_map/ppermute | solution.py:20
  17.3 79.8 %collective-permute-start.1 = (bf16[1,1024,256]{2,1,0:T(8,128)(2,1)}, bf16[1,1024,256]{2,1,0:T(8,128)(2,1)}, u32[]{:S(2)}, u32[]{:S(2)}) collective-permute-start(bf16[1,1024,256]{2,1,0:T(8,128)(2,1)} %get-tuple-element.1655), channel_id=1, source_target_pairs={{0,3},{1,0},{2,1},{3,2},{4,7},{5,4},{6,5},{7,6},{8,11},{9,8},{10,9... | collective-permute-start | bytes 1572872 | tf_op jit(solution)/shard_map/ppermute | solution.py:23
  21.1 883.8 %reduce-scatter.12.cloned.1.call-start = ((), (), s32[]{:S(2)}) async-start(), calls=%async_computation.10 | async-start | bytes 5242880 | tf_op jit(solution)/shard_map/reduce_scatter | solution.py:203
  25.2 116.7 %copy-start.82 = (f32[1,1024]{1,0:T(1,128)}, f32[1,1024]{1,0:T(1,128)S(1)}, u32[]{:S(2)}) copy-start(f32[1,1024]{1,0:T(1,128)S(1)} %get-tuple-element.1694) | copy-start | bytes 12292
  25.2 116.7 %copy-start.84 = (f32[1,1024]{1,0:T(1,128)}, f32[1,1024]{1,0:T(1,128)S(1)}, u32[]{:S(2)}) copy-start(f32[1,1024]{1,0:T(1,128)S(1)} %get-tuple-element.1695) | copy-start | bytes 12292
  25.2 116.7 %copy-start.86 = (f32[1,1024]{1,0:T(1,128)}, f32[1,1024]{1,0:T(1,128)S(1)}, u32[]{:S(2)}) copy-start(f32[1,1024]{1,0:T(1,128)S(1)} %get-tuple-element.1696) | copy-start | bytes 12292
  25.3 116.7 %copy-start.88 = (f32[1,1024]{1,0:T(1,128)}, f32[1,1024]{1,0:T(1,128)S(1)}, u32[]{:S(2)}) copy-start(f32[1,1024]{1,0:T(1,128)S(1)} %get-tuple-element.1720) | copy-start | bytes 12292
  35.6 73.4 %collective-permute-start.5 = (bf16[1,1024,256]{2,1,0:T(8,128)(2,1)}, bf16[1,1024,256]{2,1,0:T(8,128)(2,1)}, u32[]{:S(2)}, u32[]{:S(2)}) collective-permute-start(bf16[1,1024,256]{2,1,0:T(8,128)(2,1)} %collective-permute-done.3), channel_id=1, source_target_pairs={{0,1},{1,2},{2,3},{3,0},{4,5},{5,6},{6,7},{7,4},{8,9},{9,10},{10,1... | collective-permute-start | bytes 1572872 | tf_op jit(solution)/shard_map/ppermute | solution.py:20
  55.9 261.5 %copy-start.119 = (f32[512]{0:T(512)}, f32[512]{0:T(512)S(1)}, u32[]{:S(2)}) copy-start(f32[512]{0:T(512)S(1)} %mul.2320) | copy-start | bytes 6148
  74.8 49.8 %collective-permute-start.2 = (bf16[1,1024,256]{2,1,0:T(8,128)(2,1)}, bf16[1,1024,256]{2,1,0:T(8,128)(2,1)S(1)}, u32[]{:S(2)}, u32[]{:S(2)}) collective-permute-start(bf16[1,1024,256]{2,1,0:T(8,128)(2,1)} %collective-permute-done), channel_id=1, source_target_pairs={{0,1},{1,2},{2,3},{3,0},{4,5},{5,6},{6,7},{7,4},{8,9},{9,10},{10,1... | collective-permute-start | bytes 1572872 | tf_op jit(solution)/shard_map/ppermute | solution.py:20
  147.1 229.3 %copy-start.1 = (f32[1,1024,512]{2,1,0:T(8,128)}, f32[1,1024,512]{2,1,0:T(8,128)S(1)}, u32[]{:S(2)}) copy-start(f32[1,1024,512]{2,1,0:T(8,128)S(1)} %get-tuple-element.1592) | copy-start | bytes 6291460
  346.8 558.1 %reduce-scatter.10.cloned.1.call-start = ((), (), s32[]{:S(2)}) async-start(), calls=%async_computation.9 | async-start | bytes 5242880 | tf_op jit(solution)/shard_map/reduce_scatter | solution.py:203
  352.3 555.5 %reduce-scatter.16.cloned.1.call-start = ((), (), s32[]{:S(2)}) async-start(), calls=%async_computation.14 | async-start | bytes 5242880 | tf_op jit(solution)/shard_map/reduce_scatter | solution.py:232
  727.6 211.1 %reduce-scatter.14.cloned.1.call-start = ((), (), s32[]{:S(2)}) async-start(), calls=%async_computation.12 | async-start | bytes 5242880 | tf_op jit(solution)/shard_map/reduce_scatter | solution.py:232
  735.4 250.5 %reduce-scatter.24.cloned.1.call-start = ((), (), s32[]{:S(2)}) async-start(), calls=%async_computation.18 | async-start | bytes 36864 | tf_op jit(solution)/shard_map/reduce_scatter | solution.py:260
  875.1 138.4 %reduce-scatter.22.cloned.1.call-start = ((), (), s32[]{:S(2)}) async-start(), calls=%async_computation.17 | async-start | bytes 1179648 | tf_op jit(solution)/shard_map/reduce_scatter | solution.py:259
  878.3 180.7 %reduce-scatter.26.cloned.1.call-start = ((), (), s32[]{:S(2)}) async-start(), calls=%async_computation.19 | async-start | bytes 2359296 | tf_op jit(solution)/shard_map/reduce_scatter | solution.py:261
  884.9 219.0 %reduce-scatter.20.cloned.1.call-start = ((), (), s32[]{:S(2)}) async-start(), calls=%async_computation.16 | async-start | bytes 2359296 | tf_op jit(solution)/shard_map/reduce_scatter | solution.py:258
  890.8 258.6 %reduce-scatter.18.cloned.1.call-start = ((), (), s32[]{:S(2)}) async-start(), calls=%async_computation.15 | async-start | bytes 2359296 | tf_op jit(solution)/shard_map/reduce_scatter | solution.py:257
  (256 other events, 2679.8 us)
Sparse Core Ops, SparseCore 0:
  9.8 84.8 all-gather.4
  96.3 59.7 all-gather.2
  346.9 77.0 reduce-scatter.11
  426.3 77.2 reduce-scatter.9
  727.7 130.9 reduce-scatter.15
  860.9 77.6 reduce-scatter.13
  942.2 31.0 reduce-scatter.23
  977.4 36.0 reduce-scatter.21
  1017.7 41.2 reduce-scatter.25
  1062.7 41.2 reduce-scatter.19
  1108.1 41.2 reduce-scatter.17
